TPU v7x, 32 devices: a whole 2x2x4 slice. The times are simulated.
32 devices in a mesh: row: 16 (over z, y, core), col: 2 (over x).
Axes of the slice: x: 2, y: 2, z: 4, core: 2. Of those that a mesh axis runs over, the one named last changes fastest.
Arguments:
- factor: float32 [49152, 8192], P('row', 'col'), may hold values from -0.0390625 to 0.0390625
- covariance: float32 [49152, 2048], P('row', 'col'), may hold values from -6 to 6
- inv_diagonal: float32 [8192], P(('col', 'row')), may hold values from 0.5 to 4
- columns: int32 [2048], replicated, may hold values from 0 to 8191
Outputs:
- sigma_window: float32 [8192, 2048], P(('col', 'row'))
Inputs may be any that keep to these rules, and one draw needn't show every extreme that they name: `columns`: each entry is a separator index; entries may repeat.
All inputs are finite; a program needn't handle non-finite values.
Results may differ from a plain program's by a relative error of at most 0.000071.
Values sent between devices are 32-bit elements; how exact they have to be, the bound alone decides.
A program may use at most 192 MiB of HBM per device.

v0:
```python
import jax
import jax.numpy as jnp
from jax import lax
from jax.sharding import PartitionSpec as P


def contract_rows(left_block, right_block):
    return lax.dot_general(
        left_block,
        right_block,
        (((0,), (0,)), ((), ())),
        precision=lax.Precision.HIGHEST,
        preferred_element_type=jnp.float32,
    )


def per_device(factor, covariance, inv_diagonal, columns):
    row_devices = lax.axis_size("row")
    gathered = lax.all_gather(covariance, "col", axis=1, tiled=True)
    product = lax.psum_scatter(
        contract_rows(factor, gathered), "row", scatter_dimension=0, tiled=True
    )
    row_count = product.shape[0]
    block_index = lax.axis_index("col") * row_devices + lax.axis_index("row")
    row_ids = block_index * row_count + lax.iota(jnp.int32, row_count)
    on_diagonal = row_ids[:, None] == columns[None, :]
    return jnp.where(on_diagonal, inv_diagonal[:, None], jnp.zeros((), jnp.float32)) - product


def solution(mesh):
    return jax.shard_map(
        per_device,
        mesh=mesh,
        in_specs=(P("row", "col"), P("row", "col"), P(("col", "row")), P()),
        out_specs=P(("col", "row"), None),
        check_vma=False,
    )
```

profile of v0, /device:TPU:0, one launch (start us, length us, event | category | flops | bytes accessed | tf_op | source)
XLA Modules:
  0.0 970.9 jit_solution(3923775901115452385)
XLA Ops:
  6.5 0.0 all-gather.2.cloned.1.call-start
  6.5 0.7 all-gather.2.cloned.1.call-update
  7.3 0.0 reduce-scatter.2.cloned.1.call-start
  7.3 298.0 %all-gather.2.cloned.1.call-done = f32[3072,2048]{1,0:T(8,128)} async-done(((f32[3072,1024]{1,0:T(8,128)}), f32[3072,2048]{1,0:T(8,128)}) %all-gather.2.cloned.1.call-update) | async-done | bytes 25165840 | tf_op jit(solution)/shard_map/all_gather | solution.py:19
  305.4 322.6 %fusion = f32[4096,2048]{1,0:T(8,128)} fusion(f32[3072,4096]{1,0:T(8,128)} %param.4, f32[3072,2048]{1,0:T(8,128)} %all-gather.2.cloned.1.call-done), kind=kOutput, calls=%fused_computation.2 | convolution fusion | flops 309237645312 | bytes 109051904 | tf_op jit(solution)/shard_map/dot_general | solution.py:8
  627.9 0.0 copy-start
  627.9 0.0 copy-start.1
  627.9 0.0 reduce-scatter.2.cloned.1.call-update
  628.0 332.9 %reduce-scatter.2.cloned.1.call-done = f32[256,2048]{1,0:T(8,128)} async-done(((f32[4096,2048]{1,0:T(8,128)}), f32[256,2048]{1,0:T(8,128)}) %reduce-scatter.2.cloned.1.call-update) | async-done | bytes 2097168 | tf_op jit(solution)/shard_map/reduce_scatter | solution.py:20
  960.9 0.0 copy-done
  960.9 0.0 copy-done.1
  960.9 3.2 select_subtract_fusion
  (1 shorter events, 0.0 us)
Async XLA Ops:
  6.5 298.8 %all-gather.2.cloned.1.call-start = ((), (), s32[]{:S(2)}) async-start(), calls=%async_computation.1 | async-start | bytes 37748736 | tf_op jit(solution)/shard_map/all_gather | solution.py:19
  7.3 953.6 %reduce-scatter.2.cloned.1.call-start = ((), (), s32[]{:S(2)}) async-start(), calls=%async_computation.2 | async-start | bytes 35651584 | tf_op jit(solution)/shard_map/reduce_scatter | solution.py:20
  627.9 332.9 %copy-start = (s32[2048]{0:T(1024)S(1)}, s32[2048]{0:T(1024)}, u32[]{:S(2)}) copy-start(s32[2048]{0:T(1024)} %param.7) | copy-start | bytes 24580
  627.9 332.9 %copy-start.1 = (f32[256]{0:T(256)S(1)}, f32[256]{0:T(256)}, u32[]{:S(2)}) copy-start(f32[256]{0:T(256)} %param.6) | copy-start | bytes 3076
Sparse Core Ops, SparseCore 0:
  8.9 296.3 all-gather.1
  628.1 332.7 reduce-scatter.1
where the time goes:
time: 971 us
  waiting for transfers between devices  632 us (65%)
  matrix products  323 us (33%)
  between operations  13.4 us (1%)
    reduce_scatter x1, waiting for transfers between devices, per_device(): lax.psum_scatter(contract_rows(factor, gathered), 'row', scatter_dimensio...  333 us
    dot_general x1, matrix products, contract_rows(): lax.dot_general(left_block, right_block, (((0,), (0,)), ((), ())), precis...  323 us
    all_gather x1, waiting for transfers between devices, per_device(): gathered = lax.all_gather(covariance, 'col', axis=1, tiled=True)  298 us
  transfers between devices with their start and end apart: 2, of which 2 were waited for; matrix products, arithmetic and copies ran while one was open for 0% of the time, Pallas kernels for 0%

commit v1 on v0

v1 whole, which is shorter than its diff:
```python
import jax
import jax.numpy as jnp
from jax import lax
from jax.experimental.layout import Layout, with_layout_constraint
from jax.sharding import PartitionSpec as P


def contract_rows(left_block, right_block):
    return lax.dot_general(
        left_block,
        right_block,
        (((0,), (0,)), ((), ())),
        precision=lax.Precision.HIGH,
        preferred_element_type=jnp.float32,
    )


def widths(total, parts):
    unit = total // 8
    if unit % 128:
        return [total]
    return [unit * part for part in parts]


def per_device(factor, covariance, inv_diagonal, columns):
    row_devices, col_devices = lax.axis_size("row"), lax.axis_size("col")
    row, col = lax.axis_index("row"), lax.axis_index("col")
    width = covariance.shape[1]
    row_count = inv_diagonal.shape[0]
    core = lax.rem(row, 2)
    chips = row_devices // 2
    pairs = [(i, i ^ 1) for i in range(row_devices)]
    groups = [[2 * chip + side for chip in range(chips)] for side in range(2)]
    row_ids = (col * row_devices + row) * row_count + lax.iota(jnp.int32, row_count)

    def reduced(block, pair=()):
        partial = with_layout_constraint(contract_rows(factor, block), Layout((0, 1)))
        if pair:
            partial, *here = lax.optimization_barrier((partial, *[received[at] for at in pair]))
            for at, value in zip(pair, here):
                received[at] = value
        partial = partial.reshape(chips, 2, row_count, -1)
        give = lax.dynamic_index_in_dim(partial, 1 - core, 1, keepdims=False)
        keep = lax.dynamic_index_in_dim(partial, core, 1, keepdims=False)
        chip_sum = keep + lax.ppermute(give, "row", pairs)
        chip_sum = chip_sum.reshape(chips * row_count, -1)
        return lax.psum_scatter(
            chip_sum, "row", scatter_dimension=0, axis_index_groups=groups, tiled=True
        )

    def columns_of(start, size):
        return lax.slice_in_dim(covariance, start, start + size, axis=1)

    begins, received = [], []
    for step in range(1, col_devices):
        owner = lax.rem(col - step + col_devices, col_devices)
        shift = [(i, (i + step) % col_devices) for i in range(col_devices)]
        start = 0
        for size in widths(width, (1,) * 8):
            block = columns_of(start, size)
            if len(received) >= 2:
                block, received[-2] = lax.optimization_barrier((block, received[-2]))
            begins.append(owner * width + start)
            received.append(lax.ppermute(block, "col", shift))
            start += size

    own_parts = widths(width, (4, 4))
    owned, start = [], 0
    for size in own_parts:
        owned.append((col * width + start, columns_of(start, size)))
        start += size
    together = 2 if len(own_parts) > 1 else 1
    pairs_at = [
        list(range(first, first + together)) for first in range(0, len(received), together)
    ]

    def after(entry, pair):
        begin, block = entry
        block, *here = lax.optimization_barrier((block, *[received[at] for at in pair]))
        for at, value in zip(pair, here):
            received[at] = value
        return begin, block

    def taken(*chosen):
        return [(begins[at], received[at]) for pair in chosen for at in pair]

    waits_for = {}
    if len(own_parts) > 1 and len(pairs_at) > 3:
        plan = [[owned[0]], [after(owned[1], pairs_at[0])], taken(pairs_at[0], pairs_at[1])]
        plan += pairs_at[2:]
        waits_for = dict(enumerate(pairs_at))
    else:
        plan = [[entry] for entry in owned] + pairs_at

    out = jnp.zeros((row_count, columns.shape[0]), jnp.float32)
    for index, entries in enumerate(plan):
        if isinstance(entries[0], int):
            entries = taken(entries)
        product = reduced(
            jnp.concatenate([block for _, block in entries], axis=1),
            waits_for.get(index, ()),
        )
        start = 0
        for begin, block in entries:
            size = block.shape[1]
            ids = lax.dynamic_slice_in_dim(columns, begin, size)
            on_diagonal = row_ids[:, None] == ids[None, :]
            diagonal = jnp.where(on_diagonal, inv_diagonal[:, None], jnp.zeros((), jnp.float32))
            window = diagonal - lax.slice_in_dim(product, start, start + size, axis=1)
            out = lax.dynamic_update_slice(out, window, (0, begin))
            start += size
    return out


def solution(mesh):
    return jax.shard_map(
        per_device,
        mesh=mesh,
        in_specs=(P("row", "col"), P("row", "col"), P(("col", "row")), P()),
        out_specs=P(("col", "row"), None),
        check_vma=False,
    )
```

time: 971 us -> 540 us (0.56)
  waiting for transfers between devices: 632 us -> 198 us
  matrix products: 323 us -> 251 us
  local copies, waits for them, and re-layouts: 0.01 us -> 32.4 us
  other arithmetic: 3.19 us -> 26.1 us
  starting transfers between devices: 0.04 us -> 9.76 us
    all_gather x1 -> x0, waiting for transfers between devices: 298 us -> none  [per_device(): gathered = lax.all_gather(covariance, 'col', axis=1, tiled=True)]
    reduce_scatter x1 -> x5, waiting for transfers between devices: 333 us -> 116 us  [reduced(): lax.psum_scatter(chip_sum, 'row', scatter_dimension=0, axis_index_groups=...]
    ppermute x0 -> x13, waiting for transfers between devices: none -> 82.3 us  [the longest x8 54.3 us: per_device(): received.append(lax.ppermute(block, 'col', shift))]
    dot_general x1 -> x5, matrix products: 323 us -> 251 us  [contract_rows(): lax.dot_general(left_block, right_block, (((0,), (0,)), ((), ())), precis...]
    add x1 -> x6, other arithmetic: 0.01 us -> 15.8 us  [the longest x5 15.8 us: reduced(): chip_sum = keep + lax.ppermute(give, 'row', pairs)]
    slice x0 -> x2, local copies, waits for them, and re-layouts: none -> 14.7 us  [columns_of(): return lax.slice_in_dim(covariance, start, start + size, axis=1)]
    squeeze x0 -> x5, local copies, waits for them, and re-layouts: none -> 14.6 us  [reduced(): give = lax.dynamic_index_in_dim(partial, 1 - core, 1, keepdims=False)]
    dynamic_update_slice x0 -> x10, other arithmetic: none -> 10.3 us  [per_device(): out = lax.dynamic_update_slice(out, window, (0, begin))]
  transfers between devices with their start and end apart: 2 -> 18, of which waited for: 2 -> 11; matrix products, arithmetic and copies ran while one was open for 0% -> 55% of each run, Pallas kernels for 0% -> 0%
where the time goes in v1:
time: 540 us; the launch traced here: 531 us
  matrix products  251 us (46%)
  waiting for transfers between devices  198 us (37%)
  local copies, waits for them, and re-layouts  32.4 us (6%)
  other arithmetic  26.1 us (5%)
  between operations  13.6 us (3%)
  starting transfers between devices  9.76 us (2%)
    dot_general x5, matrix products, contract_rows(): lax.dot_general(left_block, right_block, (((0,), (0,)), ((), ())), precis...  251 us
    reduce_scatter x5, waiting for transfers between devices, reduced(): lax.psum_scatter(chip_sum, 'row', scatter_dimension=0, axis_index_groups=...  116 us
    ppermute x8, waiting for transfers between devices, per_device(): received.append(lax.ppermute(block, 'col', shift))  54.3 us
    ppermute x5, waiting for transfers between devices, reduced(): chip_sum = keep + lax.ppermute(give, 'row', pairs)  27.9 us
    add x5, other arithmetic, reduced(): chip_sum = keep + lax.ppermute(give, 'row', pairs)  15.8 us
    slice x2, local copies, waits for them, and re-layouts, columns_of(): return lax.slice_in_dim(covariance, start, start + size, axis=1)  14.7 us
    squeeze x5, local copies, waits for them, and re-layouts, reduced(): give = lax.dynamic_index_in_dim(partial, 1 - core, 1, keepdims=False)  14.6 us
  transfers between devices with their start and end apart: 18, of which 11 were waited for; matrix products, arithmetic and copies ran while one was open for 55% of the time, Pallas kernels for 0%

profile of v1, /device:TPU:0, one launch (start us, length us, event | category | flops | bytes accessed | tf_op | source)
XLA Modules:
  0.0 531.0 jit_solution(4386999041581609571)
XLA Ops:
  6.5 8.5 %fusion.27 = (f32[3072,128]{1,0:T(8,128)S(1)}, f32[3072,128]{1,0:T(8,128)}, f32[3072,128]{1,0:T(8,128)}, f32[3072,128]{1,0:T(8,128)}, f32[3072,128]{1,0:T(8,128)...) fusion(f32[3072,1024]{1,0:T(8,128)} %param.5), kind=kLoop, calls=%fused_computation.51 | loop fusion | bytes 25165824 | tf_op jit(solution)/shard_map/slice | solution.py:52
  15.1 2.9 collective-permute-start
  18.0 47.8 %fusion.7 = f32[4096,512]{1,0:T(8,128)} fusion(f32[3072,4096]{1,0:T(8,128)} %param.4, f32[3072,1024]{1,0:T(8,128)} %param.5), kind=kOutput, calls=%fused_computation.9 | convolution fusion | flops 38654705664 | bytes 65011712 | tf_op jit(solution)/shard_map/dot_general | solution.py:9
  65.8 6.2 %slice.55 = f32[3072,512]{1,0:T(8,128)} slice(f32[3072,1024]{1,0:T(8,128)} %param.5), slice={[0:3072], [512:1024]} | slice | bytes 12582912 | tf_op jit(solution)/shard_map/slice | solution.py:52
  72.0 14.4 %collective-permute-done.1 = f32[3072,128]{1,0:T(8,128)} collective-permute-done((f32[3072,128]{1,0:T(8,128)}, f32[3072,128]{1,0:T(8,128)}, u32[]{:S(2)}, u32[]{:S(2)}) %collective-permute-start.1) | collective-permute-done | bytes 1572896 | tf_op jit(solution)/shard_map/ppermute | solution.py:64
  86.4 4.6 dynamic-slice_bitcast_fusion.2
  91.0 1.7 collective-permute-start.3
  93.0 5.5 %collective-permute-done.2 = f32[8,256,512]{2,1,0:T(8,128)} collective-permute-done((f32[8,256,512]{2,1,0:T(8,128)}, f32[8,256,512]{2,1,0:T(8,128)}, u32[]{:S(2)}, u32[]{:S(2)}) %collective-permute-start.2) | collective-permute-done | bytes 4194336 | tf_op jit(solution)/shard_map/ppermute | solution.py:45
  98.5 6.4 %bitcast_add_fusion.2 = f32[8,256,512]{2,1,0:T(8,128)} fusion(f32[8,256,512]{2,1,0:T(8,128)} %collective-permute-done.2, f32[8,2,256,512]{3,2,1,0:T(8,128)} %bitcast.54, s32[]{:T(128)S(6)} %select_n.90), kind=kLoop, calls=%fused_computation.14 | loop fusion | flops 1048576 | bytes 12582916 | tf_op jit(solution)/shard_map/add | solution.py:45
  105.0 47.5 %convolution_bitcast_fusion.1 = f32[4096,512]{1,0:T(8,128)} fusion(f32[3072,512]{1,0:T(8,128)} %slice.55, f32[3072,4096]{1,0:T(8,128)} %param.4), kind=kOutput, calls=%fused_computation.1 | convolution fusion | flops 38654705664 | bytes 65011712 | tf_op jit(solution)/shard_map/dot_general | solution.py:9
  152.6 9.3 %collective-permute-done.4 = f32[3072,128]{1,0:T(8,128)} collective-permute-done((f32[3072,128]{1,0:T(8,128)}, f32[3072,128]{1,0:T(8,128)}, u32[]{:S(2)}, u32[]{:S(2)}) %collective-permute-start.4) | collective-permute-done | bytes 1572896 | tf_op jit(solution)/shard_map/ppermute | solution.py:64
  161.8 3.1 dynamic-slice_bitcast_fusion.1
  165.0 7.1 %collective-permute-done.5 = f32[8,256,512]{2,1,0:T(8,128)S(1)} collective-permute-done((f32[8,256,512]{2,1,0:T(8,128)S(1)}, f32[8,256,512]{2,1,0:T(8,128)S(1)}, u32[]{:S(2)}, u32[]{:S(2)}) %collective-permute-start.5) | collective-permute-done | bytes 4194336 | tf_op jit(solution)/shard_map/ppermute | solution.py:45
  172.2 3.0 bitcast_add_fusion.1
  175.2 1.8 collective-permute-start.6
  177.3 56.3 %convolution_bitcast_fusion = f32[4096,512]{1,0:T(8,128)} fusion(f32[3072,4096]{1,0:T(8,128)} %param.4, f32[3072,128]{1,0:T(8,128)} %collective-permute-done.4, f32[3072,128]{1,0:T(8,128)} %collective-permute-done.3, f32[3072,128]{1,0:T(8,128)} %collective-permute-done.1, f32[3072,128]{1,0:T(8,128)} %collective-permute-done), kind=kOutput, calls=%fused_computation | convolution fusion | flops 38659424256 | bytes 65011712 | tf_op jit(solution)/shard_map/dot_general | solution.py:9
  233.6 12.1 %collective-permute-done.7 = f32[3072,128]{1,0:T(8,128)} collective-permute-done((f32[3072,128]{1,0:T(8,128)}, f32[3072,128]{1,0:T(8,128)}, u32[]{:S(2)}, u32[]{:S(2)}) %collective-permute-start.7) | collective-permute-done | bytes 1572896 | tf_op jit(solution)/shard_map/ppermute | solution.py:64
  245.8 3.1 dynamic-slice_bitcast_fusion
  248.9 7.1 %collective-permute-done.8 = f32[8,256,512]{2,1,0:T(8,128)S(1)} collective-permute-done((f32[8,256,512]{2,1,0:T(8,128)S(1)}, f32[8,256,512]{2,1,0:T(8,128)S(1)}, u32[]{:S(2)}, u32[]{:S(2)}) %collective-permute-start.8) | collective-permute-done | bytes 4194336 | tf_op jit(solution)/shard_map/ppermute | solution.py:45
  256.1 3.0 bitcast_add_fusion
  259.1 1.8 collective-permute-start.10
  261.2 49.7 %convolution_bitcast_fusion.2 = f32[4096,256]{1,0:T(8,128)} fusion(f32[3072,4096]{1,0:T(8,128)} %param.4, f32[3072,128]{1,0:T(8,128)} %collective-permute-done.7, f32[3072,128]{1,0:T(8,128)} %collective-permute-done.6), kind=kOutput, calls=%fused_computation.11 | convolution fusion | flops 19328139264 | bytes 57671680 | tf_op jit(solution)/shard_map/dot_general | solution.py:9
  310.9 18.5 %collective-permute-done.9 = f32[3072,128]{1,0:T(8,128)} collective-permute-done((f32[3072,128]{1,0:T(8,128)S(1)}, f32[3072,128]{1,0:T(8,128)}, u32[]{:S(2)}, u32[]{:S(2)}) %collective-permute-start.9) | collective-permute-done | bytes 1572896 | tf_op jit(solution)/shard_map/ppermute | solution.py:64
  329.4 1.9 dynamic-slice_bitcast_fusion.4
  331.4 4.1 collective-permute-done.11
  335.6 1.7 bitcast_add_fusion.4
  337.3 49.4 %fusion.12 = f32[256,4096]{0,1:T(8,128)} fusion(f32[3072,4096]{1,0:T(8,128)} %param.4, f32[3072,128]{1,0:T(8,128)} %collective-permute-done.10, f32[3072,128]{1,0:T(8,128)} %collective-permute-done.9), kind=kOutput, calls=%fused_computation.21 | convolution fusion | flops 19328139264 | bytes 57671680 | tf_op jit(solution)/shard_map/dot_general | solution.py:9
  386.8 1.9 dynamic-slice_bitcast_fusion.3
  388.9 4.0 collective-permute-done.12
  402.1 47.7 %reduce-scatter.12.cloned.1.call-done = f32[256,256]{1,0:T(8,128)} async-done(((f32[2048,256]{1,0:T(8,128)}), f32[256,256]{1,0:T(8,128)}) %reduce-scatter.12.cloned.1.call-update) | async-done | bytes 262160 | tf_op jit(solution)/shard_map/reduce_scatter | solution.py:47
  451.9 68.4 %reduce-scatter.14.cloned.1.call-done = f32[256,256]{1,0:T(8,128)} async-done(((f32[2048,256]{1,0:T(8,128)}), f32[256,256]{1,0:T(8,128)}) %reduce-scatter.14.cloned.1.call-update) | async-done | bytes 262160 | tf_op jit(solution)/shard_map/reduce_scatter | solution.py:47
  522.6 1.7 fusion.16
  (56 shorter events, 15.0 us)
Async XLA Ops:
  6.5 388.9 %reduce-scatter.6.cloned.1.call-start = ((), (), s32[]{:S(2)}) async-start(), calls=%async_computation.5 | async-start | bytes 4718592 | tf_op jit(solution)/shard_map/reduce_scatter | solution.py:47
  15.1 56.9 %collective-permute-start = (f32[3072,128]{1,0:T(8,128)}, f32[3072,128]{1,0:T(8,128)}, u32[]{:S(2)}, u32[]{:S(2)}) collective-permute-start(f32[3072,128]{1,0:T(8,128)} %get-tuple-element.56), channel_id=1, source_target_pairs={{0,1},{1,0},{2,3},{3,2},{4,5},{5,4},{6,7},{7,6},{8,9},{9,8},{10,11... | collective-permute-start | bytes 4718600 | tf_op jit(solution)/shard_map/ppermute | solution.py:64
  18.0 68.4 %collective-permute-start.1 = (f32[3072,128]{1,0:T(8,128)}, f32[3072,128]{1,0:T(8,128)}, u32[]{:S(2)}, u32[]{:S(2)}) collective-permute-start(f32[3072,128]{1,0:T(8,128)} %get-tuple-element.54), channel_id=1, source_target_pairs={{0,1},{1,0},{2,3},{3,2},{4,5},{5,4},{6,7},{7,6},{8,9},{9,8},{10,11... | collective-permute-start | bytes 4718600 | tf_op jit(solution)/shard_map/ppermute | solution.py:64
  91.0 7.5 %collective-permute-start.2 = (f32[8,256,512]{2,1,0:T(8,128)}, f32[8,256,512]{2,1,0:T(8,128)}, u32[]{:S(2)}, u32[]{:S(2)}) collective-permute-start(f32[8,256,512]{2,1,0:T(8,128)} %dynamic-slice_bitcast_fusion.2), channel_id=1, source_target_pairs={{0,2},{2,0},{4,6},{6,4},{8,10},{10,8},{12,14},{14,12},{16,18},{18,... | collective-permute-start | bytes 12582920 | tf_op jit(solution)/shard_map/ppermute | solution.py:45
  91.0 61.6 %collective-permute-start.3 = (f32[3072,128]{1,0:T(8,128)}, f32[3072,128]{1,0:T(8,128)}, u32[]{:S(2)}, u32[]{:S(2)}) collective-permute-start(f32[3072,128]{1,0:T(8,128)} %get-tuple-element.34), channel_id=1, source_target_pairs={{0,1},{1,0},{2,3},{3,2},{4,5},{5,4},{6,7},{7,6},{8,9},{9,8},{10,11... | collective-permute-start | bytes 4718600 | tf_op jit(solution)/shard_map/ppermute | solution.py:64
  92.7 69.1 %collective-permute-start.4 = (f32[3072,128]{1,0:T(8,128)}, f32[3072,128]{1,0:T(8,128)}, u32[]{:S(2)}, u32[]{:S(2)}) collective-permute-start(f32[3072,128]{1,0:T(8,128)} %get-tuple-element.36), channel_id=1, source_target_pairs={{0,1},{1,0},{2,3},{3,2},{4,5},{5,4},{6,7},{7,6},{8,9},{9,8},{10,11... | collective-permute-start | bytes 4718600 | tf_op jit(solution)/shard_map/ppermute | solution.py:64
  105.0 291.7 %reduce-scatter.8.cloned.1.call-start = ((), (), s32[]{:S(2)}) async-start(), calls=%async_computation.6 | async-start | bytes 4718592 | tf_op jit(solution)/shard_map/reduce_scatter | solution.py:47
  161.8 10.3 %copy-start.3 = (f32[4096,512]{1,0:T(8,128)S(1)}, f32[4096,512]{1,0:T(8,128)}, u32[]{:S(2)}) copy-start(f32[4096,512]{1,0:T(8,128)} %convolution_bitcast_fusion.1) | copy-start | bytes 25165828
  164.9 7.2 %collective-permute-start.5 = (f32[8,256,512]{2,1,0:T(8,128)S(1)}, f32[8,256,512]{2,1,0:T(8,128)S(1)}, u32[]{:S(2)}, u32[]{:S(2)}) collective-permute-start(f32[8,256,512]{2,1,0:T(8,128)S(1)} %dynamic-slice_bitcast_fusion.1), channel_id=1, source_target_pairs={{0,2},{2,0},{4,6},{6,4},{8,10},{10,8},{12,14},{14,12},{16,18},{18,... | collective-permute-start | bytes 12582920 | tf_op jit(solution)/shard_map/ppermute | solution.py:45
  175.2 222.7 %reduce-scatter.10.cloned.1.call-start = ((), (), s32[]{:S(2)}) async-start(), calls=%async_computation.7 | async-start | bytes 4718592 | tf_op jit(solution)/shard_map/reduce_scatter | solution.py:47
  175.2 58.4 %collective-permute-start.6 = (f32[3072,128]{1,0:T(8,128)}, f32[3072,128]{1,0:T(8,128)}, u32[]{:S(2)}, u32[]{:S(2)}) collective-permute-start(f32[3072,128]{1,0:T(8,128)} %get-tuple-element.39), channel_id=1, source_target_pairs={{0,1},{1,0},{2,3},{3,2},{4,5},{5,4},{6,7},{7,6},{8,9},{9,8},{10,11... | collective-permute-start | bytes 4718600 | tf_op jit(solution)/shard_map/ppermute | solution.py:64
  177.0 68.7 %collective-permute-start.7 = (f32[3072,128]{1,0:T(8,128)}, f32[3072,128]{1,0:T(8,128)}, u32[]{:S(2)}, u32[]{:S(2)}) collective-permute-start(f32[3072,128]{1,0:T(8,128)} %get-tuple-element.41), channel_id=1, source_target_pairs={{0,1},{1,0},{2,3},{3,2},{4,5},{5,4},{6,7},{7,6},{8,9},{9,8},{10,11... | collective-permute-start | bytes 4718600 | tf_op jit(solution)/shard_map/ppermute | solution.py:64
  245.8 10.3 %copy-start.2 = (f32[4096,512]{1,0:T(8,128)S(1)}, f32[4096,512]{1,0:T(8,128)}, u32[]{:S(2)}) copy-start(f32[4096,512]{1,0:T(8,128)} %convolution_bitcast_fusion) | copy-start | bytes 25165828
  248.9 7.2 %collective-permute-start.8 = (f32[8,256,512]{2,1,0:T(8,128)S(1)}, f32[8,256,512]{2,1,0:T(8,128)S(1)}, u32[]{:S(2)}, u32[]{:S(2)}) collective-permute-start(f32[8,256,512]{2,1,0:T(8,128)S(1)} %dynamic-slice_bitcast_fusion), channel_id=1, source_target_pairs={{0,2},{2,0},{4,6},{6,4},{8,10},{10,8},{12,14},{14,12},{16,18},{18,... | collective-permute-start | bytes 12582920 | tf_op jit(solution)/shard_map/ppermute | solution.py:45
  259.1 190.7 %reduce-scatter.12.cloned.1.call-start = ((), (), s32[]{:S(2)}) async-start(), calls=%async_computation.8 | async-start | bytes 2359296 | tf_op jit(solution)/shard_map/reduce_scatter | solution.py:47
  259.1 51.8 %collective-permute-start.10 = (f32[3072,128]{1,0:T(8,128)S(1)}, f32[3072,128]{1,0:T(8,128)}, u32[]{:S(2)}, u32[]{:S(2)}) collective-permute-start(f32[3072,128]{1,0:T(8,128)S(1)} %get-tuple-element.47), channel_id=1, source_target_pairs={{0,1},{1,0},{2,3},{3,2},{4,5},{5,4},{6,7},{7,6},{8,9},{9,8},{10,11... | collective-permute-start | bytes 4718600 | tf_op jit(solution)/shard_map/ppermute | solution.py:64
  260.9 68.5 %collective-permute-start.9 = (f32[3072,128]{1,0:T(8,128)S(1)}, f32[3072,128]{1,0:T(8,128)}, u32[]{:S(2)}, u32[]{:S(2)}) collective-permute-start(f32[3072,128]{1,0:T(8,128)S(1)} %get-tuple-element.46), channel_id=1, source_target_pairs={{0,1},{1,0},{2,3},{3,2},{4,5},{5,4},{6,7},{7,6},{8,9},{9,8},{10,11... | collective-permute-start | bytes 4718600 | tf_op jit(solution)/shard_map/ppermute | solution.py:64
  329.4 6.2 %copy-start = (f32[4096,256]{1,0:T(8,128)S(1)}, f32[4096,256]{1,0:T(8,128)}, u32[]{:S(2)}) copy-start(f32[4096,256]{1,0:T(8,128)} %convolution_bitcast_fusion.2) | copy-start | bytes 12582916
  331.4 4.2 collective-permute-start.11
  337.3 182.9 %reduce-scatter.14.cloned.1.call-start = ((), (), s32[]{:S(2)}) async-start(), calls=%async_computation.9 | async-start | bytes 2359296 | tf_op jit(solution)/shard_map/reduce_scatter | solution.py:47
  386.8 6.1 %copy-start.1 = (f32[256,4096]{0,1:T(8,128)S(1)}, f32[256,4096]{0,1:T(8,128)}, u32[]{:S(2)}) copy-start(f32[256,4096]{0,1:T(8,128)} %fusion.12) | copy-start | bytes 12582916
  388.7 4.2 collective-permute-start.12
  394.6 0.7 copy-start.7
  394.6 1.1 copy-start.6
  395.5 1.0 copy-start.5
  521.3 1.3 copy-start.4
Sparse Core Ops, SparseCore 0:
  105.1 89.5 reduce-scatter.5
  198.7 87.6 reduce-scatter.7
  290.1 87.6 reduce-scatter.9
  381.6 68.1 reduce-scatter.11
  453.6 66.6 reduce-scatter.13

commit v2 on v0

v2 whole, which is shorter than its diff:
```python
import jax
import jax.numpy as jnp
from jax import lax
from jax.experimental.layout import Layout, with_layout_constraint
from jax.sharding import PartitionSpec as P


def contract_rows(left_block, right_block):
    return lax.dot_general(
        left_block,
        right_block,
        (((0,), (0,)), ((), ())),
        precision=lax.Precision.HIGH,
        preferred_element_type=jnp.float32,
    )


def widths(total, parts):
    unit = total // 8
    if unit % 128:
        return [total]
    return [unit * part for part in parts]


def per_device(factor, covariance, inv_diagonal, columns):
    row_devices, col_devices = lax.axis_size("row"), lax.axis_size("col")
    row, col = lax.axis_index("row"), lax.axis_index("col")
    width = covariance.shape[1]
    row_count = inv_diagonal.shape[0]
    row_ids = (col * row_devices + row) * row_count + lax.iota(jnp.int32, row_count)

    def halved(total, stride):
        side = lax.rem(row // stride, 2)
        halves = total.reshape(total.shape[0] // 2, 2, row_count, -1)
        give = lax.dynamic_index_in_dim(halves, 1 - side, 1, keepdims=False)
        keep = lax.dynamic_index_in_dim(halves, side, 1, keepdims=False)
        swap = [(i, i ^ stride) for i in range(row_devices)]
        return keep + lax.ppermute(give, "row", swap)

    def columns_of(start, size):
        return lax.slice_in_dim(covariance, start, start + size, axis=1)

    parts = widths(width, (1,) * 8)
    together = 2 if len(parts) > 1 else 1
    coming = []
    for step in range(1, col_devices):
        owner = lax.rem(col - step + col_devices, col_devices)
        shift = [(i, (i + step) % col_devices) for i in range(col_devices)]
        start = 0
        for size in parts:
            coming.append((owner * width + start, start, size, shift))
            start += size
    pairs = [coming[first : first + together] for first in range(0, len(coming), together)]
    owned, start = [], 0
    for size in widths(width, (4, 4)):
        owned.append((col * width + start, columns_of(start, size)))
        start += size

    received, sums, strides, plan = [], [], [], []

    def advance():
        for at in range(len(sums)):
            if strides[at] < row_devices:
                sums[at] = halved(sums[at], strides[at])
                strides[at] *= 2

    def multiply(entries, ready, pair):
        block = jnp.concatenate([block for _, block in entries], axis=1)
        if ready:
            block = lax.optimization_barrier((block, *ready))[0]
        partial = with_layout_constraint(contract_rows(factor, block), Layout((0, 1)))
        if pair:
            partial, *pair = lax.optimization_barrier((partial, *pair))
        plan.append([(begin, block.shape[1]) for begin, block in entries])
        sums.append(partial.reshape(row_devices, row_count, -1))
        strides.append(1)
        return pair

    waiting = owned
    for index, pair in enumerate(pairs):
        ready = [total for total, stride in zip(sums, strides) if 1 < stride < row_devices]
        advance()
        blocks = [columns_of(start, size) for _, start, size, _ in pair]
        if received:
            ready = ready + received
        if ready:
            blocks = lax.optimization_barrier((*blocks, *ready))[: len(blocks)]
        arriving = [lax.ppermute(block, "col", entry[3]) for block, entry in zip(blocks, pair)]
        if index == 1 and len(waiting) == 1:
            begin, block = waiting[0]
            waiting = [(begin, lax.optimization_barrier((block, *received))[0])]
        if index < len(owned):
            taken, waiting = waiting[:1], waiting[1:]
        else:
            taken, waiting = waiting, []
        arriving = multiply(taken, [], arriving)
        waiting = waiting + [(entry[0], block) for entry, block in zip(pair, arriving)]
        received = arriving
    ready = [total for total, stride in zip(sums, strides) if 1 < stride < 8]
    sums[-1], strides[-1] = halved(sums[-1], 1), 2
    ready.append(sums[-1])
    advance()
    beside = [at for at in range(len(sums)) if strides[at] == 4]
    for at, total in zip(beside, multiply(waiting, ready, [sums[at] for at in beside])):
        sums[at] = total
    while min(strides) < row_devices:
        advance()

    out = jnp.zeros((row_count, columns.shape[0]), jnp.float32)
    for entries, total in zip(plan, sums):
        product = total.reshape(row_count, -1)
        start = 0
        for begin, size in entries:
            ids = lax.dynamic_slice_in_dim(columns, begin, size)
            on_diagonal = row_ids[:, None] == ids[None, :]
            diagonal = jnp.where(on_diagonal, inv_diagonal[:, None], jnp.zeros((), jnp.float32))
            window = diagonal - lax.slice_in_dim(product, start, start + size, axis=1)
            out = lax.dynamic_update_slice(out, window, (0, begin))
            start += size
    return out


def solution(mesh):
    return jax.shard_map(
        per_device,
        mesh=mesh,
        in_specs=(P("row", "col"), P("row", "col"), P(("col", "row")), P()),
        out_specs=P(("col", "row"), None),
        check_vma=False,
    )
```

time: 971 us -> 551 us (0.57)
  waiting for transfers between devices: 632 us -> 189 us
  matrix products: 323 us -> 248 us
  local copies, waits for them, and re-layouts: 0.01 us -> 41.4 us
  other arithmetic: 3.19 us -> 33.9 us
  starting transfers between devices: 0.04 us -> 28.2 us
  between operations: 13.4 us -> 0.8 us
    reduce_scatter x1 -> x0, waiting for transfers between devices: 333 us -> none  [per_device(): lax.psum_scatter(contract_rows(factor, gathered), 'row', scatter_dimensio...]
    all_gather x1 -> x0, waiting for transfers between devices: 298 us -> none  [per_device(): gathered = lax.all_gather(covariance, 'col', axis=1, tiled=True)]
    ppermute x0 -> x28, waiting for transfers between devices: none -> 189 us  [the longest x20 120 us: halved(): return keep + lax.ppermute(give, 'row', swap)]
    dot_general x1 -> x5, matrix products: 323 us -> 248 us  [contract_rows(): lax.dot_general(left_block, right_block, (((0,), (0,)), ((), ())), precis...]
    add x1 -> x16, other arithmetic: 0.01 us -> 29.6 us  [the longest x15 29.6 us: halved(): return keep + lax.ppermute(give, 'row', swap)]
    ppermute x0 -> x28, starting transfers between devices: none -> 28.2 us  [the longest x20 19 us: halved(): return keep + lax.ppermute(give, 'row', swap)]
    squeeze x0 -> x20, local copies, waits for them, and re-layouts: none -> 27.4 us  [halved(): give = lax.dynamic_index_in_dim(halves, 1 - side, 1, keepdims=False)]
  transfers between devices with their start and end apart: 2 -> 28, of which waited for: 2 -> 10; matrix products, arithmetic and copies ran while one was open for 0% -> 56% of each run, Pallas kernels for 0% -> 0%
where the time goes in v2:
time: 551 us; the launch traced here: 541 us
  matrix products  248 us (45%)
  waiting for transfers between devices  189 us (34%)
  local copies, waits for them, and re-layouts  41.4 us (8%)
  other arithmetic  33.9 us (6%)
  starting transfers between devices  28.2 us (5%)
    dot_general x5, matrix products, contract_rows(): lax.dot_general(left_block, right_block, (((0,), (0,)), ((), ())), precis...  248 us
    ppermute x20, waiting for transfers between devices, halved(): return keep + lax.ppermute(give, 'row', swap)  120 us
    ppermute x8, waiting for transfers between devices, per_device(): lax.ppermute(block, 'col', entry[3])  68.8 us
    add x15, other arithmetic, halved(): return keep + lax.ppermute(give, 'row', swap)  29.6 us
    squeeze x20, local copies, waits for them, and re-layouts, halved(): give = lax.dynamic_index_in_dim(halves, 1 - side, 1, keepdims=False)  27.4 us
    ppermute x20, starting transfers between devices, halved(): return keep + lax.ppermute(give, 'row', swap)  19 us
  transfers between devices with their start and end apart: 28, of which 10 were waited for; matrix products, arithmetic and copies ran while one was open for 56% of the time, Pallas kernels for 0%

profile of v2, /device:TPU:0, one launch (start us, length us, event | category | flops | bytes accessed | tf_op | source)
XLA Modules:
  0.0 541.4 jit_solution(11956085936341503554)
XLA Ops:
  0.0 8.5 %fusion.26 = (f32[3072,128]{1,0:T(8,128)}, f32[3072,128]{1,0:T(8,128)}, f32[3072,128]{1,0:T(8,128)}, f32[3072,128]{1,0:T(8,128)S(1)}, f32[3072,128]{1,0:T(8,128)...) fusion(f32[3072,1024]{1,0:T(8,128)} %param.5), kind=kLoop, calls=%fused_computation.79 | loop fusion | bytes 25165824 | tf_op jit(solution)/shard_map/slice | solution.py:41
  8.5 2.9 collective-permute-start
  11.5 47.5 %fusion.9 = f32[4096,512]{1,0:T(8,128)} fusion(f32[3072,4096]{1,0:T(8,128)} %param.4, f32[3072,1024]{1,0:T(8,128)} %param.5), kind=kOutput, calls=%fused_computation.10 | convolution fusion | flops 38654705664 | bytes 65011712 | tf_op jit(solution)/shard_map/dot_general | solution.py:9
  59.0 20.8 %collective-permute-done.1 = f32[3072,128]{1,0:T(8,128)} collective-permute-done((f32[3072,128]{1,0:T(8,128)}, f32[3072,128]{1,0:T(8,128)}, u32[]{:S(2)}, u32[]{:S(2)}) %collective-permute-start.1) | collective-permute-done | bytes 1572896 | tf_op jit(solution)/shard_map/ppermute | solution.py:88
  79.8 4.7 dynamic-slice_bitcast_fusion.2
  86.6 58.1 %fusion.7 = f32[4096,512]{1,0:T(8,128)} fusion(f32[3072,4096]{1,0:T(8,128)} %param.4, f32[3072,1024]{1,0:T(8,128)} %param.5), kind=kOutput, calls=%fused_computation.8 | convolution fusion | flops 38654705664 | bytes 65011712 | tf_op jit(solution)/shard_map/dot_general | solution.py:9
  144.8 10.4 %collective-permute-done.7 = f32[3072,128]{1,0:T(8,128)} collective-permute-done((f32[3072,128]{1,0:T(8,128)S(1)}, f32[3072,128]{1,0:T(8,128)}, u32[]{:S(2)}, u32[]{:S(2)}) %collective-permute-start.7) | collective-permute-done | bytes 1572896 | tf_op jit(solution)/shard_map/ppermute | solution.py:88
  155.2 4.9 dynamic-slice_bitcast_fusion.1
  161.4 3.2 bitcast_add_fusion.2
  168.7 47.6 %convolution_bitcast_fusion = f32[4096,512]{1,0:T(8,128)} fusion(f32[3072,4096]{1,0:T(8,128)} %param.4, f32[3072,128]{1,0:T(8,128)} %collective-permute-done.7, f32[3072,128]{1,0:T(8,128)} %collective-permute-done.6, f32[3072,128]{1,0:T(8,128)} %collective-permute-done.1, f32[3072,128]{1,0:T(8,128)} %collective-permute-done), kind=kOutput, calls=%fused_computation | convolution fusion | flops 38659424256 | bytes 65011712 | tf_op jit(solution)/shard_map/dot_general | solution.py:9
  216.2 18.4 %collective-permute-done.13 = f32[3072,128]{1,0:T(8,128)} collective-permute-done((f32[3072,128]{1,0:T(8,128)}, f32[3072,128]{1,0:T(8,128)}, u32[]{:S(2)}, u32[]{:S(2)}) %collective-permute-start.13) | collective-permute-done | bytes 1572896 | tf_op jit(solution)/shard_map/ppermute | solution.py:88
  234.7 4.6 dynamic-slice_bitcast_fusion
  239.3 4.5 bitcast_add_fusion.1
  248.7 2.1 bitcast_add_fusion.7
  252.9 49.4 %convolution_bitcast_fusion.2 = f32[4096,256]{1,0:T(8,128)} fusion(f32[3072,4096]{1,0:T(8,128)} %param.4, f32[3072,128]{1,0:T(8,128)} %collective-permute-done.13, f32[3072,128]{1,0:T(8,128)} %collective-permute-done.12), kind=kOutput, calls=%fused_computation.13 | convolution fusion | flops 19328139264 | bytes 57671680 | tf_op jit(solution)/shard_map/dot_general | solution.py:9
  302.3 19.1 %collective-permute-done.15 = f32[3072,128]{1,0:T(8,128)} collective-permute-done((f32[3072,128]{1,0:T(8,128)}, f32[3072,128]{1,0:T(8,128)}, u32[]{:S(2)}, u32[]{:S(2)}) %collective-permute-start.15) | collective-permute-done | bytes 1572896 | tf_op jit(solution)/shard_map/ppermute | solution.py:88
  321.4 3.1 dynamic-slice_bitcast_fusion.5
  327.1 2.1 pad_maximum_fusion
  329.2 2.2 bitcast_add_fusion.6
  333.6 2.0 bitcast_add_fusion.5
  338.3 4.5 bitcast_add_fusion
  345.9 45.7 %convolution_bitcast_fusion.1 = f32[4096,256]{1,0:T(8,128)} fusion(f32[3072,256]{1,0:T(8,128)S(1)} %pad_maximum_fusion, f32[3072,4096]{1,0:T(8,128)} %param.4), kind=kOutput, calls=%fused_computation.12 | convolution fusion | flops 19327352832 | bytes 57671680 | tf_op jit(solution)/shard_map/dot_general | solution.py:9
  393.4 13.9 %collective-permute-done.18 = f32[4,256,512]{2,1,0:T(8,128)} collective-permute-done((f32[4,256,512]{2,1,0:T(8,128)}, f32[4,256,512]{2,1,0:T(8,128)}, u32[]{:S(2)}, u32[]{:S(2)}) %collective-permute-start.18) | collective-permute-done | bytes 2097184 | tf_op jit(solution)/shard_map/ppermute | solution.py:38
  407.3 4.1 bitcast_add_fusion.4
  418.4 2.7 collective-permute-start.5
  423.0 50.9 %collective-permute-done.22 = f32[2,256,256]{2,1,0:T(8,128)S(1)} collective-permute-done((f32[2,256,256]{2,1,0:T(8,128)S(1)}, f32[2,256,256]{2,1,0:T(8,128)S(1)}, u32[]{:S(2)}, u32[]{:S(2)}) %collective-permute-start.22) | collective-permute-done | bytes 524320 | tf_op jit(solution)/shard_map/ppermute | solution.py:38
  475.1 2.2 collective-permute-start.21
  477.3 2.0 bitcast_add_fusion.3
  481.6 18.1 %collective-permute-done.23 = f32[1,256,256]{2,1,0:T(8,128)S(1)} collective-permute-done((f32[1,256,256]{2,1,0:T(8,128)S(1)}, f32[1,256,256]{2,1,0:T(8,128)S(1)}, u32[]{:S(2)}, u32[]{:S(2)}) %collective-permute-start.23) | collective-permute-done | bytes 262176 | tf_op jit(solution)/shard_map/ppermute | solution.py:38
  499.7 11.0 %collective-permute-done.21 = f32[1,256,512]{2,1,0:T(8,128)S(1)} collective-permute-done((f32[1,256,512]{2,1,0:T(8,128)S(1)}, f32[1,256,512]{2,1,0:T(8,128)S(1)}, u32[]{:S(2)}, u32[]{:S(2)}) %collective-permute-start.21) | collective-permute-done | bytes 524320 | tf_op jit(solution)/shard_map/ppermute | solution.py:38
  511.7 13.3 %collective-permute-done.26 = f32[2,256,256]{2,1,0:T(8,128)S(1)} collective-permute-done((f32[2,256,256]{2,1,0:T(8,128)S(1)}, f32[2,256,256]{2,1,0:T(8,128)S(1)}, u32[]{:S(2)}, u32[]{:S(2)}) %collective-permute-start.26) | collective-permute-done | bytes 524320 | tf_op jit(solution)/shard_map/ppermute | solution.py:38
  526.1 12.8 %collective-permute-done.27 = f32[1,256,256]{2,1,0:T(8,128)S(1)} collective-permute-done((f32[1,256,256]{2,1,0:T(8,128)S(1)}, f32[1,256,256]{2,1,0:T(8,128)S(1)}, u32[]{:S(2)}, u32[]{:S(2)}) %collective-permute-start.27) | collective-permute-done | bytes 262176 | tf_op jit(solution)/shard_map/ppermute | solution.py:38
  (119 shorter events, 43.4 us)
Async XLA Ops:
  8.5 50.5 %collective-permute-start = (f32[3072,128]{1,0:T(8,128)}, f32[3072,128]{1,0:T(8,128)}, u32[]{:S(2)}, u32[]{:S(2)}) collective-permute-start(f32[3072,128]{1,0:T(8,128)} %get-tuple-element.55), channel_id=1, source_target_pairs={{0,1},{1,0},{2,3},{3,2},{4,5},{5,4},{6,7},{7,6},{8,9},{9,8},{10,11... | collective-permute-start | bytes 4718600 | tf_op jit(solution)/shard_map/ppermute | solution.py:88
  11.4 68.4 %collective-permute-start.1 = (f32[3072,128]{1,0:T(8,128)}, f32[3072,128]{1,0:T(8,128)}, u32[]{:S(2)}, u32[]{:S(2)}) collective-permute-start(f32[3072,128]{1,0:T(8,128)} %get-tuple-element.54), channel_id=1, source_target_pairs={{0,1},{1,0},{2,3},{3,2},{4,5},{5,4},{6,7},{7,6},{8,9},{9,8},{10,11... | collective-permute-start | bytes 4718600 | tf_op jit(solution)/shard_map/ppermute | solution.py:88
  84.6 75.6 %collective-permute-start.2 = (f32[8,256,512]{2,1,0:T(8,128)}, f32[8,256,512]{2,1,0:T(8,128)}, u32[]{:S(2)}, u32[]{:S(2)}) collective-permute-start(f32[8,256,512]{2,1,0:T(8,128)} %dynamic-slice_bitcast_fusion.2), channel_id=1, source_target_pairs={{0,2},{2,0},{4,6},{6,4},{8,10},{10,8},{12,14},{14,12},{16,18},{18,... | collective-permute-start | bytes 12582920 | tf_op jit(solution)/shard_map/ppermute | solution.py:38
  84.6 60.2 %collective-permute-start.6 = (f32[3072,128]{1,0:T(8,128)S(1)}, f32[3072,128]{1,0:T(8,128)}, u32[]{:S(2)}, u32[]{:S(2)}) collective-permute-start(f32[3072,128]{1,0:T(8,128)S(1)} %get-tuple-element.30), channel_id=1, source_target_pairs={{0,1},{1,0},{2,3},{3,2},{4,5},{5,4},{6,7},{7,6},{8,9},{9,8},{10,11... | collective-permute-start | bytes 4718600 | tf_op jit(solution)/shard_map/ppermute | solution.py:88
  86.3 68.9 %collective-permute-start.7 = (f32[3072,128]{1,0:T(8,128)S(1)}, f32[3072,128]{1,0:T(8,128)}, u32[]{:S(2)}, u32[]{:S(2)}) collective-permute-start(f32[3072,128]{1,0:T(8,128)S(1)} %get-tuple-element.31), channel_id=1, source_target_pairs={{0,1},{1,0},{2,3},{3,2},{4,5},{5,4},{6,7},{7,6},{8,9},{9,8},{10,11... | collective-permute-start | bytes 4718600 | tf_op jit(solution)/shard_map/ppermute | solution.py:88
  160.1 79.1 %collective-permute-start.8 = (f32[8,256,512]{2,1,0:T(8,128)}, f32[8,256,512]{2,1,0:T(8,128)}, u32[]{:S(2)}, u32[]{:S(2)}) collective-permute-start(f32[8,256,512]{2,1,0:T(8,128)} %dynamic-slice_bitcast_fusion.1), channel_id=1, source_target_pairs={{0,2},{2,0},{4,6},{6,4},{8,10},{10,8},{12,14},{14,12},{16,18},{18,... | collective-permute-start | bytes 12582920 | tf_op jit(solution)/shard_map/ppermute | solution.py:38
  164.6 51.7 %collective-permute-start.12 = (f32[3072,128]{1,0:T(8,128)}, f32[3072,128]{1,0:T(8,128)}, u32[]{:S(2)}, u32[]{:S(2)}) collective-permute-start(f32[3072,128]{1,0:T(8,128)} %get-tuple-element.35), channel_id=1, source_target_pairs={{0,1},{1,0},{2,3},{3,2},{4,5},{5,4},{6,7},{7,6},{8,9},{9,8},{10,11... | collective-permute-start | bytes 4718600 | tf_op jit(solution)/shard_map/ppermute | solution.py:88
  166.4 68.3 %collective-permute-start.13 = (f32[3072,128]{1,0:T(8,128)}, f32[3072,128]{1,0:T(8,128)}, u32[]{:S(2)}, u32[]{:S(2)}) collective-permute-start(f32[3072,128]{1,0:T(8,128)} %get-tuple-element.36), channel_id=1, source_target_pairs={{0,1},{1,0},{2,3},{3,2},{4,5},{5,4},{6,7},{7,6},{8,9},{9,8},{10,11... | collective-permute-start | bytes 4718600 | tf_op jit(solution)/shard_map/ppermute | solution.py:88
  166.9 81.8 %collective-permute-start.3 = (f32[4,256,512]{2,1,0:T(8,128)S(1)}, f32[4,256,512]{2,1,0:T(8,128)}, u32[]{:S(2)}, u32[]{:S(2)}) collective-permute-start(f32[4,256,512]{2,1,0:T(8,128)S(1)} %dynamic-slice_bitcast_fusion.7), channel_id=1, source_target_pairs={{0,4},{2,6},{4,0},{6,2},{8,12},{10,14},{12,8},{14,10},{16,20},{18,... | collective-permute-start | bytes 6291464 | tf_op jit(solution)/shard_map/ppermute | solution.py:38
  239.3 99.0 %collective-permute-start.16 = (f32[8,256,512]{2,1,0:T(8,128)}, f32[8,256,512]{2,1,0:T(8,128)}, u32[]{:S(2)}, u32[]{:S(2)}) collective-permute-start(f32[8,256,512]{2,1,0:T(8,128)} %dynamic-slice_bitcast_fusion), channel_id=1, source_target_pairs={{0,2},{2,0},{4,6},{6,4},{8,10},{10,8},{12,14},{14,12},{16,18},{18,... | collective-permute-start | bytes 12582920 | tf_op jit(solution)/shard_map/ppermute | solution.py:38
  246.9 82.3 %collective-permute-start.9 = (f32[4,256,512]{2,1,0:T(8,128)}, f32[4,256,512]{2,1,0:T(8,128)}, u32[]{:S(2)}, u32[]{:S(2)}) collective-permute-start(f32[4,256,512]{2,1,0:T(8,128)} %dynamic-slice_bitcast_fusion.6), channel_id=1, source_target_pairs={{0,4},{2,6},{4,0},{6,2},{8,12},{10,14},{12,8},{14,10},{16,20},{18,... | collective-permute-start | bytes 6291464 | tf_op jit(solution)/shard_map/ppermute | solution.py:38
  250.8 73.7 %copy-start.8 = (f32[4,256,512]{2,1,0:T(8,128)}, f32[4,256,512]{2,1,0:T(8,128)S(1)}, u32[]{:S(2)}) copy-start(f32[4,256,512]{2,1,0:T(8,128)S(1)} %bitcast_add_fusion.7) | copy-start | bytes 6291460
  250.8 51.5 %collective-permute-start.14 = (f32[3072,128]{1,0:T(8,128)}, f32[3072,128]{1,0:T(8,128)}, u32[]{:S(2)}, u32[]{:S(2)}) collective-permute-start(f32[3072,128]{1,0:T(8,128)} %get-tuple-element.39), channel_id=1, source_target_pairs={{0,1},{1,0},{2,3},{3,2},{4,5},{5,4},{6,7},{7,6},{8,9},{9,8},{10,11... | collective-permute-start | bytes 4718600 | tf_op jit(solution)/shard_map/ppermute | solution.py:88
  252.3 69.1 %collective-permute-start.15 = (f32[3072,128]{1,0:T(8,128)}, f32[3072,128]{1,0:T(8,128)}, u32[]{:S(2)}, u32[]{:S(2)}) collective-permute-start(f32[3072,128]{1,0:T(8,128)} %get-tuple-element.40), channel_id=1, source_target_pairs={{0,1},{1,0},{2,3},{3,2},{4,5},{5,4},{6,7},{7,6},{8,9},{9,8},{10,11... | collective-permute-start | bytes 4718600 | tf_op jit(solution)/shard_map/ppermute | solution.py:88
  324.4 9.1 %collective-permute-start.17 = (f32[8,256,256]{2,1,0:T(8,128)}, f32[8,256,256]{2,1,0:T(8,128)}, u32[]{:S(2)}, u32[]{:S(2)}) collective-permute-start(f32[8,256,256]{2,1,0:T(8,128)} %dynamic-slice_bitcast_fusion.5), channel_id=1, source_target_pairs={{0,2},{2,0},{4,6},{6,4},{8,10},{10,8},{12,14},{14,12},{16,18},{18,... | collective-permute-start | bytes 6291464 | tf_op jit(solution)/shard_map/ppermute | solution.py:38
  325.5 90.0 %collective-permute-start.4 = (f32[2,256,512]{2,1,0:T(8,128)}, f32[2,256,512]{2,1,0:T(8,128)}, u32[]{:S(2)}, u32[]{:S(2)}) collective-permute-start(f32[2,256,512]{2,1,0:T(8,128)} %dynamic-slice_bitcast_fusion.12), channel_id=1, source_target_pairs={{0,8},{2,10},{4,12},{6,14},{8,0},{10,2},{12,4},{14,6},{16,24},{18,... | collective-permute-start | bytes 3145736 | tf_op jit(solution)/shard_map/ppermute | solution.py:38
  332.6 88.5 %collective-permute-start.10 = (f32[2,256,512]{2,1,0:T(8,128)}, f32[2,256,512]{2,1,0:T(8,128)}, u32[]{:S(2)}, u32[]{:S(2)}) collective-permute-start(f32[2,256,512]{2,1,0:T(8,128)} %dynamic-slice_bitcast_fusion.11), channel_id=1, source_target_pairs={{0,8},{2,10},{4,12},{6,14},{8,0},{10,2},{12,4},{14,6},{16,24},{18,... | collective-permute-start | bytes 3145736 | tf_op jit(solution)/shard_map/ppermute | solution.py:38
  336.7 54.9 %collective-permute-start.19 = (f32[4,256,256]{2,1,0:T(8,128)}, f32[4,256,256]{2,1,0:T(8,128)}, u32[]{:S(2)}, u32[]{:S(2)}) collective-permute-start(f32[4,256,256]{2,1,0:T(8,128)} %dynamic-slice_bitcast_fusion.10), channel_id=1, source_target_pairs={{0,4},{2,6},{4,0},{6,2},{8,12},{10,14},{12,8},{14,10},{16,20},{18,... | collective-permute-start | bytes 3145736 | tf_op jit(solution)/shard_map/ppermute | solution.py:38
  345.3 61.9 %collective-permute-start.18 = (f32[4,256,512]{2,1,0:T(8,128)}, f32[4,256,512]{2,1,0:T(8,128)}, u32[]{:S(2)}, u32[]{:S(2)}) collective-permute-start(f32[4,256,512]{2,1,0:T(8,128)} %dynamic-slice_bitcast_fusion.4), channel_id=1, source_target_pairs={{0,4},{2,6},{4,0},{6,2},{8,12},{10,14},{12,8},{14,10},{16,20},{18,... | collective-permute-start | bytes 6291464 | tf_op jit(solution)/shard_map/ppermute | solution.py:38
  393.3 18.0 %copy-start = (f32[4096,256]{1,0:T(8,128)S(1)}, f32[4096,256]{1,0:T(8,128)}, u32[]{:S(2)}) copy-start(f32[4096,256]{1,0:T(8,128)} %convolution_bitcast_fusion.1) | copy-start | bytes 12582916
  413.0 64.3 %collective-permute-start.24 = (f32[8,256,256]{2,1,0:T(8,128)}, f32[8,256,256]{2,1,0:T(8,128)}, u32[]{:S(2)}, u32[]{:S(2)}) collective-permute-start(f32[8,256,256]{2,1,0:T(8,128)} %dynamic-slice_bitcast_fusion.3), channel_id=1, source_target_pairs={{0,2},{2,0},{4,6},{6,4},{8,10},{10,8},{12,14},{14,12},{16,18},{18,... | collective-permute-start | bytes 6291464 | tf_op jit(solution)/shard_map/ppermute | solution.py:38
  414.7 6.4 %copy-start.11 = (f32[4,256,512]{2,1,0:T(8,128)S(1)}, f32[4,256,512]{2,1,0:T(8,128)}, u32[]{:S(2)}) copy-start(f32[4,256,512]{2,1,0:T(8,128)} %copy-done.10) | copy-start | bytes 6291460
  414.7 60.2 %collective-permute-start.20 = (f32[2,256,512]{2,1,0:T(8,128)S(1)}, f32[2,256,512]{2,1,0:T(8,128)S(1)}, u32[]{:S(2)}, u32[]{:S(2)}) collective-permute-start(f32[2,256,512]{2,1,0:T(8,128)S(1)} %dynamic-slice_bitcast_fusion.9), channel_id=1, source_target_pairs={{0,8},{2,10},{4,12},{6,14},{8,0},{10,2},{12,4},{14,6},{16,24},{18,... | collective-permute-start | bytes 3145736 | tf_op jit(solution)/shard_map/ppermute | solution.py:38
  417.0 56.8 %collective-permute-start.22 = (f32[2,256,256]{2,1,0:T(8,128)S(1)}, f32[2,256,256]{2,1,0:T(8,128)S(1)}, u32[]{:S(2)}, u32[]{:S(2)}) collective-permute-start(f32[2,256,256]{2,1,0:T(8,128)S(1)} %dynamic-slice_bitcast_fusion.14), channel_id=1, source_target_pairs={{0,8},{2,10},{4,12},{6,14},{8,0},{10,2},{12,4},{14,6},{16,24},{18,... | collective-permute-start | bytes 1572872 | tf_op jit(solution)/shard_map/ppermute | solution.py:38
  418.4 62.6 %collective-permute-start.5 = (f32[1,256,512]{2,1,0:T(8,128)S(1)}, f32[1,256,512]{2,1,0:T(8,128)S(1)}, u32[]{:S(2)}, u32[]{:S(2)}) collective-permute-start(f32[1,256,512]{2,1,0:T(8,128)S(1)} %constant_dynamic-slice_fusion.4), channel_id=1, source_target_pairs={{0,16},{2,18},{4,20},{6,22},{8,24},{10,26},{12,28},{14,30},{16,0},... | collective-permute-start | bytes 1572872 | tf_op jit(solution)/shard_map/ppermute | solution.py:38
  422.5 52.4 %copy-start.12 = (f32[4,256,512]{2,1,0:T(8,128)S(1)}, f32[4,256,512]{2,1,0:T(8,128)}, u32[]{:S(2)}) copy-start(f32[4,256,512]{2,1,0:T(8,128)} %bitcast_add_fusion.4) | copy-start | bytes 6291460
  422.6 58.8 %collective-permute-start.11 = (f32[1,256,512]{2,1,0:T(8,128)S(1)}, f32[1,256,512]{2,1,0:T(8,128)S(1)}, u32[]{:S(2)}, u32[]{:S(2)}) collective-permute-start(f32[1,256,512]{2,1,0:T(8,128)S(1)} %constant_dynamic-slice_fusion.3), channel_id=1, source_target_pairs={{0,16},{2,18},{4,20},{6,22},{8,24},{10,26},{12,28},{14,30},{16,0},... | collective-permute-start | bytes 1572872 | tf_op jit(solution)/shard_map/ppermute | solution.py:38
  474.0 25.7 %collective-permute-start.23 = (f32[1,256,256]{2,1,0:T(8,128)S(1)}, f32[1,256,256]{2,1,0:T(8,128)S(1)}, u32[]{:S(2)}, u32[]{:S(2)}) collective-permute-start(f32[1,256,256]{2,1,0:T(8,128)S(1)} %constant_dynamic-slice_fusion.1), channel_id=1, source_target_pairs={{0,16},{2,18},{4,20},{6,22},{8,24},{10,26},{12,28},{14,30},{16,0},... | collective-permute-start | bytes 786440 | tf_op jit(solution)/shard_map/ppermute | solution.py:38
  475.1 35.5 %collective-permute-start.21 = (f32[1,256,512]{2,1,0:T(8,128)S(1)}, f32[1,256,512]{2,1,0:T(8,128)S(1)}, u32[]{:S(2)}, u32[]{:S(2)}) collective-permute-start(f32[1,256,512]{2,1,0:T(8,128)S(1)} %constant_dynamic-slice_fusion.2), channel_id=1, source_target_pairs={{0,16},{2,18},{4,20},{6,22},{8,24},{10,26},{12,28},{14,30},{16,0},... | collective-permute-start | bytes 1572872 | tf_op jit(solution)/shard_map/ppermute | solution.py:38
  479.4 31.5 %collective-permute-start.25 = (f32[4,256,256]{2,1,0:T(8,128)S(1)}, f32[4,256,256]{2,1,0:T(8,128)S(1)}, u32[]{:S(2)}, u32[]{:S(2)}) collective-permute-start(f32[4,256,256]{2,1,0:T(8,128)S(1)} %dynamic-slice_bitcast_fusion.8), channel_id=1, source_target_pairs={{0,4},{2,6},{4,0},{6,2},{8,12},{10,14},{12,8},{14,10},{16,20},{18,... | collective-permute-start | bytes 3145736 | tf_op jit(solution)/shard_map/ppermute | solution.py:38
  511.2 13.8 %collective-permute-start.26 = (f32[2,256,256]{2,1,0:T(8,128)S(1)}, f32[2,256,256]{2,1,0:T(8,128)S(1)}, u32[]{:S(2)}, u32[]{:S(2)}) collective-permute-start(f32[2,256,256]{2,1,0:T(8,128)S(1)} %dynamic-slice_bitcast_fusion.13), channel_id=1, source_target_pairs={{0,8},{2,10},{4,12},{6,14},{8,0},{10,2},{12,4},{14,6},{16,24},{18,... | collective-permute-start | bytes 1572872 | tf_op jit(solution)/shard_map/ppermute | solution.py:38
  525.1 13.8 %collective-permute-start.27 = (f32[1,256,256]{2,1,0:T(8,128)S(1)}, f32[1,256,256]{2,1,0:T(8,128)S(1)}, u32[]{:S(2)}, u32[]{:S(2)}) collective-permute-start(f32[1,256,256]{2,1,0:T(8,128)S(1)} %constant_dynamic-slice_fusion), channel_id=1, source_target_pairs={{0,16},{2,18},{4,20},{6,22},{8,24},{10,26},{12,28},{14,30},{16,0},... | collective-permute-start | bytes 786440 | tf_op jit(solution)/shard_map/ppermute | solution.py:38
  (14 other events, 44.8 us)
